TPU v7x, 32 devices: a whole 2x2x4 slice. The times are simulated.
32 devices in a mesh: rep: 2 (over x), dp: 8 (over z, y), tensor: 2 (over core).
Axes of the slice: x: 2, y: 2, z: 4, core: 2. Of those that a mesh axis runs over, the one named last changes fastest.
Arguments:
- tokens: bfloat16 [7168, 8192], P(('rep', 'dp'), 'tensor'), parts along dimension 0, may hold values from -6 to 6
- value_weight: bfloat16 [8192, 1024], P('tensor'), may hold values from -0.0625 to 0.0625
- pool_down: bfloat16 [8, 8192, 64], P('dp', 'tensor'), may hold values from -0.0625 to 0.0625
- pool_up: bfloat16 [8, 64, 1024], P('dp'), may hold values from -0.75 to 0.75
- block_adapter: int32 [1792, 1], P(('rep', 'dp')), parts along dimension 0, may hold values from 0 to 7; in each aligned block of 112 rows (0 to 111, 112 to 223, ...) at most 14 rows name the same one
- pool_slot: int32 [8], replicated, may hold values from 0 to 7, each once
Outputs:
- values: bfloat16 [7168, 1024], P(('rep', 'dp'), 'tensor'), parts along dimension 0
There are 2 independent parts, one for each index of `rep`. A program takes and returns all parts, laid end to end along the dimension named above; an argument that names none is the same for every part. Nothing has to cross between parts.
Inputs may be any that keep to these rules, and one draw needn't show every extreme that they name: `block_adapter`: among the 112 blocks of one index of dp no adapter is named more than 14 times, a bound that some block reaches in them. `pool_slot`: A permutation of the pool rows.
All inputs are finite; a program needn't handle non-finite values.
Results may differ from a plain program's by a relative error of at most 0.001.
Values may be sent and summed in bfloat16 or wider, within the bound.
A program may use at most 64 MiB of HBM per device.

v0:
```python
import jax
import jax.numpy as jnp
from jax import lax
from jax.sharding import PartitionSpec as P


def shards(tokens, value_weight, pool_down, pool_up, block_adapter, pool_slot):
    peers = lax.axis_size("dp")
    cores = lax.axis_size("tensor")
    core = lax.axis_index("tensor")
    blocks = block_adapter.shape[0]
    width = tokens.shape[1]
    rows_in = tokens.shape[0] // blocks
    kv_full = value_weight.shape[1]
    kv_part = kv_full // cores
    most = max(2, (blocks + peers - 1) // peers)
    adapters = pool_slot.shape[0]
    ident = jnp.arange(adapters, dtype=jnp.int32)
    owner = jnp.sum(jnp.where(block_adapter == ident[None, :], pool_slot[None, :], 0), axis=1)
    same = owner[:, None] == owner[None, :]
    position = jnp.arange(blocks, dtype=jnp.int32)
    earlier = position[:, None] > position[None, :]
    rank_in = jnp.sum(jnp.where(same & earlier, 1, 0), axis=1)
    target = owner * most + rank_in
    flat_blocks = tokens.reshape(blocks, rows_in * width)
    outgoing = jnp.zeros((peers * most, rows_in * width), jnp.bfloat16).at[target].set(flat_blocks)
    outgoing = outgoing.reshape(peers, most * rows_in, width)
    base = jnp.dot(tokens, value_weight, preferred_element_type=jnp.float32)
    shrink_part = jnp.einsum(
        "pkd,dr->pkr",
        lax.all_to_all(outgoing, "dp", split_axis=0, concat_axis=0, tiled=True),
        pool_down[0],
        preferred_element_type=jnp.float32,
    )
    shrink_all = lax.psum(shrink_part, "tensor")
    columns = lax.dynamic_slice_in_dim(pool_up[0], core * kv_part, kv_part, 1).astype(jnp.float32)
    term = jnp.einsum("pkr,rc->pkc", shrink_all, columns, precision=lax.Precision.HIGHEST)
    answers = lax.all_to_all(term, "dp", split_axis=0, concat_axis=0, tiled=True)
    out_cols = answers.shape[2]
    answers = answers.reshape(peers * most, rows_in * out_cols)
    gathered = jnp.take(answers, target, axis=0).reshape(tokens.shape[0], out_cols)
    summed = lax.psum_scatter(base, "tensor", scatter_dimension=1, tiled=True)
    result = summed + gathered
    return result.astype(jnp.bfloat16)


def solution(mesh):
    in_specs = (
        P(("rep", "dp"), "tensor"),
        P("tensor", None),
        P("dp", "tensor", None),
        P("dp", None, None),
        P(("rep", "dp"), None),
        P(),
    )
    out_specs = P(("rep", "dp"), "tensor")
    return jax.shard_map(shards, mesh=mesh, in_specs=in_specs, out_specs=out_specs, check_vma=False)
```

profile of v0, /device:TPU:0, one launch (start us, length us, event | category | flops | bytes accessed | tf_op | source)
XLA Modules:
  0.0 181.8 jit_solution(5363384950082171352)
XLA Ops:
  6.5 0.0 copy-start
  6.5 0.0 all-reduce.2.cloned.1.call-start
  6.5 0.8 select_reduce_fusion.1
  7.4 0.2 select_reduce_fusion
  7.5 7.3 %reshape.63 = bf16[112,16384]{1,0:T(8,128)(2,1)} reshape(bf16[448,4096]{1,0:T(8,128)(2,1)} %param.6) | data formatting | bytes 7340032 | tf_op jit(solution)/shard_map/reshape | solution.py:25
  14.9 9.0 %scatter_custom_fusion = bf16[112,16384]{1,0:T(8,128)(2,1)} fusion(s32[112]{0:T(128)S(1)} %fusion.8, bf16[112,16384]{1,0:T(8,128)(2,1)} %reshape.63, bf16[]{:T(256)} %constant.15.clone.1), kind=kCustom, calls=%fused_computation.2 | custom fusion | bytes 3670528 | tf_op jit(solution)/shard_map/scatter | solution.py:26
  23.8 7.3 %reshape.49 = bf16[8,56,4096]{2,1,0:T(8,128)(2,1)} reshape(bf16[112,16384]{1,0:T(8,128)(2,1)} %scatter_custom_fusion) | data formatting | bytes 7340032 | tf_op jit(solution)/shard_map/reshape | solution.py:27
  31.1 89.2 %all_to_all.10 = bf16[8,56,4096]{2,1,0:T(8,128)(2,1)S(1)} all-to-all(bf16[8,56,4096]{2,1,0:T(8,128)(2,1)} %reshape.49), channel_id=1, replica_groups=mesh['rep'=2,'dp'=8,'tensor'=2] {'dp'}, dimensions={0} | all-to-all | bytes 7340032 | tf_op jit(solution)/shard_map/all_to_all | solution.py:31
  120.4 0.0 copy-done
  120.4 1.9 %fusion.2 = f32[8,56,64]{2,1,0:T(8,128)} fusion(bf16[8,56,4096]{2,1,0:T(8,128)(2,1)S(1)} %all_to_all.10, bf16[1,4096,64]{1,2,0:T(8,128)(2,1)S(1)} %copy-done), kind=kOutput, calls=%fused_computation.5 | convolution fusion | flops 234881024 | bytes 4308992 | tf_op jit(solution)/shard_map/pkd,dr->pkr/dot_general | solution.py:29
  122.3 0.0 all-reduce.2.cloned.1.call-update
  122.3 0.0 copy-start.1
  122.3 0.2 reduce-scatter.2.cloned.1.call-start
  122.5 9.7 %fusion.10 = f32[448,1024]{1,0:T(8,128)} fusion(bf16[448,4096]{1,0:T(8,128)(2,1)} %param.6, bf16[4096,1024]{1,0:T(8,128)(2,1)} %param.7), kind=kOutput, calls=%fused_computation.22 | convolution fusion | flops 3758096384 | bytes 13893632 | tf_op jit(solution)/shard_map/dot_general | solution.py:28
  132.2 0.0 reduce-scatter.2.cloned.1.call-update
  132.3 7.3 %all-reduce.2.cloned.1.call-done = f32[8,56,64]{2,1,0:T(8,128)} async-done(((f32[8,56,64]{2,1,0:T(8,128)}), f32[8,56,64]{2,1,0:T(8,128)}) %all-reduce.2.cloned.1.call-update) | async-done | bytes 114704 | tf_op jit(solution)/shard_map/psum | solution.py:35
  139.6 0.0 copy-done.1
  139.6 2.4 %fusion.4 = f32[8,56,512]{2,1,0:T(8,128)} fusion(f32[8,56,64]{2,1,0:T(8,128)} %all-reduce.2.cloned.1.call-done, bf16[1,64,1024]{2,1,0:T(8,128)(2,1)S(1)} %copy-done.1, s32[]{:T(128)S(6)} %select_n.37), kind=kOutput, calls=%fused_computation.7 | convolution fusion | flops 176160768 | bytes 1097732 | tf_op jit(solution)/shard_map/pkr,rc->pkc/dot_general | solution.py:37
  142.0 5.8 %all-to-all-start.1 = ((f32[8,56,512]{2,1,0:T(8,128)}), f32[8,56,512]{2,1,0:T(8,128)S(1)}, u32[]{:S(2)}, u32[]{:S(2)}) async-start(f32[8,56,512]{2,1,0:T(8,128)} %fusion.4), calls=%async_computation.2 | async-start | bytes 1835008 | tf_op jit(solution)/shard_map/all_to_all | solution.py:38
  147.8 0.1 broadcast_in_dim.48
  147.9 0.1 broadcast_in_dim.49
  148.0 23.2 %all-to-all-done.1 = f32[8,56,512]{2,1,0:T(8,128)S(1)} async-done(((f32[8,56,512]{2,1,0:T(8,128)}), f32[8,56,512]{2,1,0:T(8,128)S(1)}, u32[]{:S(2)}, u32[]{:S(2)}) %all-to-all-start.1) | async-done | bytes 917536 | tf_op jit(solution)/shard_map/all_to_all | solution.py:38
  171.2 0.4 reshape.50
  171.6 0.9 gather_fusion
  172.5 0.3 gather.7
  172.8 0.0 reduce-scatter.2.cloned.1.call-done
  172.8 2.1 %add_convert_fusion = bf16[448,512]{1,0:T(8,128)(2,1)} fusion(f32[448,512]{1,0:T(8,128)} %reduce-scatter.2.cloned.1.call-done, f32[448,512]{1,0:T(8,128)S(1)} %gather.7, pred[448]{0:T(512)(128)(4,1)S(1)} %broadcast_in_dim.49), kind=kLoop, calls=%fused_computation.4 | loop fusion | flops 688128 | bytes 2294208 | tf_op jit(solution)/shard_map/convert_element_type | solution.py:44
  (3 shorter events, 0.0 us)
Async XLA Ops:
  6.5 113.8 %copy-start = (bf16[1,4096,64]{1,2,0:T(8,128)(2,1)S(1)}, bf16[1,4096,64]{1,2,0:T(8,128)(2,1)}, u32[]{:S(2)}) copy-start(bf16[1,4096,64]{1,2,0:T(8,128)(2,1)} %param.8) | copy-start | bytes 1572868
  6.5 133.0 %all-reduce.2.cloned.1.call-start = ((), (), s32[]{:S(2)}) async-start(), calls=%async_computation.4 | async-start | bytes 458752 | tf_op jit(solution)/shard_map/psum | solution.py:35
  122.3 17.3 %copy-start.1 = (bf16[1,64,1024]{2,1,0:T(8,128)(2,1)S(1)}, bf16[1,64,1024]{2,1,0:T(8,128)(2,1)}, u32[]{:S(2)}) copy-start(bf16[1,64,1024]{2,1,0:T(8,128)(2,1)} %param.9) | copy-start | bytes 393220
  122.3 50.5 %reduce-scatter.2.cloned.1.call-start = ((), (), s32[]{:S(2)}) async-start(), calls=%async_computation.3 | async-start | bytes 2752512 | tf_op jit(solution)/shard_map/reduce_scatter | solution.py:42
  142.0 29.2 %all-to-all-start.1 = ((f32[8,56,512]{2,1,0:T(8,128)}), f32[8,56,512]{2,1,0:T(8,128)S(1)}, u32[]{:S(2)}, u32[]{:S(2)}) async-start(f32[8,56,512]{2,1,0:T(8,128)} %fusion.4), calls=%async_computation.2 | async-start | bytes 1835008 | tf_op jit(solution)/shard_map/all_to_all | solution.py:38
Sparse Core Ops, SparseCore 0:
  122.4 17.1 all-reduce.1
  141.8 10.5 reduce-scatter.1
where the time goes:
time: 182 us
  blocking collectives  89.2 us (49%)
  waiting for transfers between devices  30.6 us (17%)
  local copies, waits for them, and re-layouts  25.4 us (14%)
  matrix products  14 us (8%)
  between operations  13.5 us (7%)
  starting transfers between devices  6.01 us (3%)
  other arithmetic  3.11 us (2%)
    all_to_all x1, blocking collectives, shards(): lax.all_to_all(outgoing, 'dp', split_axis=0, concat_axis=0, tiled=True)  89.2 us
    all_to_all x1, waiting for transfers between devices, shards(): lax.all_to_all(term, 'dp', split_axis=0, concat_axis=0, tiled=True)  23.2 us
    dot_general x1, matrix products, shards(): base = jnp.dot(tokens, value_weight, preferred_element_type=jnp.float32)  9.7 us
    scatter x1, local copies, waits for them, and re-layouts, shards(): jnp.zeros((peers * most, rows_in * width), jnp.bfloat16).at[target]  8.98 us
    psum x1, waiting for transfers between devices, shards(): shrink_all = lax.psum(shrink_part, 'tensor')  7.33 us
    reshape x1, local copies, waits for them, and re-layouts, shards(): flat_blocks = tokens.reshape(blocks, rows_in * width)  7.31 us
    reshape x1, local copies, waits for them, and re-layouts, shards(): outgoing = outgoing.reshape(peers, most * rows_in, width)  7.31 us
    all_to_all x1, starting transfers between devices, shards(): lax.all_to_all(term, 'dp', split_axis=0, concat_axis=0, tiled=True)  5.78 us
  transfers between devices with their start and end apart: 3, of which 2 were waited for; matrix products, arithmetic and copies ran while one was open for 8% of the time, Pallas kernels for 0%

commit v1 on v0

--- a/solution.py
+++ b/solution.py
@@ -1,10 +1,17 @@
+import functools
+
 import jax
 import jax.numpy as jnp
 from jax import lax
+from jax.experimental import pallas as pl
+from jax.experimental.pallas import tpu as pltpu
 from jax.sharding import PartitionSpec as P
 
-
-def shards(tokens, value_weight, pool_down, pool_up, block_adapter, pool_slot):
+MESH = pl.DeviceIdType.MESH
+LINE = 4
+
+
+def moved_tokens(tokens, value_weight, pool_down, pool_up, block_adapter, pool_slot):
     peers = lax.axis_size("dp")
     cores = lax.axis_size("tensor")
     core = lax.axis_index("tensor")
@@ -44,6 +51,276 @@
     return result.astype(jnp.bfloat16)
 
 
+def kernel(tok_hbm, w_hbm, down_hbm, up_hbm, adapter_ref, slot_ref, out_ref,
+           tok, w, downs, ups, mine, other, base_in, acc, acc_in,
+           local_sem, p_recv, c_recv, u_recv, x_recv, p_send, c_send, u_send, x_send,
+           core_send, core_recv):
+    x, dp, core = lax.axis_index("rep"), lax.axis_index("dp"), lax.axis_index("tensor")
+    z, y = dp // 2, dp % 2
+    rows, width = tok.shape
+    rank = downs.shape[1]
+    half = mine.shape[1]
+    blocks = adapter_ref.shape[1]
+    rows_in = rows // blocks
+    adapters = slot_ref.shape[0]
+    third = width * 3 // 8
+    rest = width - 2 * third
+
+    own_cols = pl.ds(pl.multiple_of(x * third, 128), third)
+    far_cols = pl.ds(pl.multiple_of((1 - x) * third, 128), third)
+    rest_cols = pl.ds(2 * third, rest)
+    up_cols = pl.ds(pl.multiple_of(core * half, 128), half)
+    other_cols = pl.ds(pl.multiple_of((1 - core) * half, 128), half)
+
+    loads = [
+        pltpu.make_async_copy(tok_hbm, tok, local_sem.at[0]),
+        pltpu.make_async_copy(w_hbm.at[:, other_cols], w.at[1], local_sem.at[1]),
+        pltpu.make_async_copy(w_hbm.at[:, up_cols], w.at[0], local_sem.at[2]),
+        pltpu.make_async_copy(down_hbm, downs.at[dp], local_sem.at[3]),
+        pltpu.make_async_copy(up_hbm.at[:, up_cols], ups.at[dp], local_sem.at[4]),
+    ]
+
+    has_up, has_low = z < LINE - 1, z > 0
+    to_x, to_y, to_core = {"rep": 1 - x}, {"dp": z * 2 + 1 - y}, {"tensor": 1 - core}
+    to_up = {"dp": jnp.minimum(dp + 2, 2 * LINE - 1)}
+    to_low = {"dp": jnp.maximum(dp - 2, 0)}
+
+    barrier = pltpu.get_barrier_semaphore()
+    for near in (to_x, to_y, to_core):
+        pl.semaphore_signal(barrier, inc=1, device_id=near, device_id_type=MESH)
+
+    @pl.when(has_up)
+    def _():
+        pl.semaphore_signal(barrier, inc=1, device_id=to_up, device_id_type=MESH)
+
+    @pl.when(has_low)
+    def _():
+        pl.semaphore_signal(barrier, inc=1, device_id=to_low, device_id_type=MESH)
+
+    for load in loads:
+        load.start()
+    pl.semaphore_wait(barrier, 3 + jnp.where(has_up, 1, 0) + jnp.where(has_low, 1, 0))
+
+    def p_copy(s, way, to, own=False):
+        here = (down_hbm if own else downs.at[s]).at[:, own_cols]
+        return pltpu.make_async_remote_copy(
+            here, downs.at[s].at[:, own_cols], p_send.at[way, s], p_recv.at[s], to, MESH)
+
+    def c_copy(s, way, to, own=False):
+        here = (down_hbm if own else downs.at[s]).at[:, rest_cols]
+        return pltpu.make_async_remote_copy(
+            here, downs.at[s].at[:, rest_cols], c_send.at[way, s], c_recv.at[s], to, MESH)
+
+    def u_copy(s, way, to, own=False):
+        here = up_hbm.at[:, up_cols] if own else ups.at[s]
+        return pltpu.make_async_remote_copy(
+            here, ups.at[s], u_send.at[way, s], u_recv.at[s], to, MESH)
+
+    def x_copy(s):
+        return pltpu.make_async_remote_copy(
+            downs.at[s].at[:, own_cols], downs.at[s].at[:, own_cols], x_send.at[s], x_recv.at[s], to_x, MESH)
+
+    def x_wait(s):
+        pltpu.make_async_remote_copy(
+            downs.at[s].at[:, far_cols], downs.at[s].at[:, far_cols], x_send.at[s], x_recv.at[s], to_x, MESH).wait_recv()
+
+    def zs(s, source_z, what):
+        @pl.when(has_up & (source_z <= z))
+        def _():
+            what(0, to_up)
+
+        @pl.when(has_low & (source_z >= z))
+        def _():
+            what(1, to_low)
+
+    line = []
+    for i in range(LINE - 1):
+        rising = i + jnp.where(i >= z, 1, 0)
+        falling = LINE - 1 - (i + jnp.where(i >= LINE - 1 - z, 1, 0))
+        line.append(jnp.where(z < LINE // 2, rising, falling))
+
+    def send_p(s, source_z, own=False):
+        zs(s, source_z, lambda way, to: p_copy(s, way, to, own).start())
+        p_copy(s, 2, to_y, own).start()
+
+    def send_c(s, source_z, own=False):
+        def both(way, to):
+            c_copy(s, way, to, own).start()
+            u_copy(s, way, to, own).start()
+        zs(s, source_z, both)
+        both(2, to_y)
+
+    def got_p(s):
+        p_copy(s, 2, to_y).wait_recv()
+
+    def got_c(s):
+        c_copy(s, 2, to_y).wait_recv()
+        u_copy(s, 2, to_y).wait_recv()
+
+    near = [v * 2 + y for v in line]
+    beyond = [v * 2 + 1 - y for v in line]
+    twin = z * 2 + 1 - y
+
+    send_p(dp, z, True)
+    send_c(dp, z, True)
+
+    ids = jnp.broadcast_to(adapter_ref[...], (8, blocks))
+    own_row = jnp.zeros((8, blocks), jnp.float32)
+    for a in range(adapters):
+        own_row = own_row + jnp.where(ids == a, slot_ref[a].astype(jnp.float32), 0.0)
+    t_at = lax.broadcasted_iota(jnp.int32, (rows, blocks), 0)
+    b_at = lax.broadcasted_iota(jnp.int32, (rows, blocks), 1) * rows_in
+    spread = jnp.where((t_at >= b_at) & (t_at < b_at + rows_in), 1.0, 0.0).astype(jnp.bfloat16)
+    owner = lax.dot_general(spread, own_row.astype(jnp.bfloat16), (((1,), (1,)), ((), ())),
+                            preferred_element_type=jnp.float32)[:, :1]
+
+    def dot_cols(s, cols):
+        d = downs[s, :, cols]
+        both = jnp.concatenate([d, d], axis=0)
+        return lax.dot_general(tok[:, cols], both, (((1,), (1,)), ((), ())),
+                               preferred_element_type=jnp.float32)
+
+    def add(s, cols):
+        acc[...] += jnp.where(owner == s.astype(jnp.float32), dot_cols(s, cols), 0.0)
+
+    everything = pl.ds(0, width)
+    step = width // 8
+
+    def base(into, which):
+        into[...] = jnp.dot(tok[:, :step], w[which, :step, :], preferred_element_type=jnp.float32)
+
+        def body(k, _):
+            at = pl.ds(pl.multiple_of(k * step, step), step)
+            into[...] += jnp.dot(tok[:, at], w[which, at, :], preferred_element_type=jnp.float32)
+            return 0
+        lax.fori_loop(1, 8, body, 0)
+
+    acc[...] = jnp.zeros_like(acc)
+    for load in loads:
+        load.wait()
+
+    got_p(near[0])
+    send_p(near[0], line[0])
+    x_copy(near[0]).start()
+    got_p(twin)
+    x_copy(twin).start()
+    base(other, 1)
+    base_copy = pltpu.make_async_remote_copy(other, base_in, core_send.at[0], core_recv.at[0], to_core, MESH)
+    base_copy.start()
+    got_c(near[0])
+    send_c(near[0], line[0])
+    base(mine, 0)
+
+    got_p(near[1])
+    send_p(near[1], line[1])
+    x_copy(near[1]).start()
+    add(dp, everything)
+    got_c(twin)
+    got_p(beyond[0])
+    x_copy(beyond[0]).start()
+    got_c(near[1])
+    send_c(near[1], line[1])
+    x_wait(near[0])
+    add(near[0], everything)
+
+    got_p(near[2])
+    send_p(near[2], line[2])
+    x_copy(near[2]).start()
+    got_p(beyond[1])
+    x_copy(beyond[1]).start()
+    got_c(near[2])
+    send_c(near[2], line[2])
+    x_wait(twin)
+    add(twin, everything)
+    x_wait(near[1])
+    add(near[1], everything)
+    got_p(beyond[2])
+    x_copy(beyond[2]).start()
+
+    got_c(beyond[0])
+    x_wait(beyond[0])
+    add(beyond[0], everything)
+    x_wait(near[2])
+    add(near[2], everything)
+    got_c(beyond[1])
+    x_wait(beyond[1])
+    add(beyond[1], everything)
+    add(beyond[2], own_cols)
+    base_copy.wait()
+    mine[...] += base_in[...]
+    got_c(beyond[2])
+    add(beyond[2], rest_cols)
+    x_wait(beyond[2])
+    add(beyond[2], far_cols)
+
+    acc_copy = pltpu.make_async_remote_copy(acc, acc_in, core_send.at[1], core_recv.at[1], to_core, MESH)
+    acc_copy.start()
+
+    def sent(s, source_z, own=False):
+        def each(way, to):
+            p_copy(s, way, to, own).wait_send()
+            c_copy(s, way, to, own).wait_send()
+            u_copy(s, way, to, own).wait_send()
+        zs(s, source_z, each)
+        each(2, to_y)
+
+    sent(dp, z, True)
+    for s, v in zip(near, line):
+        sent(s, v)
+    for s in near + beyond + [twin]:
+        x_copy(s).wait_send()
+
+    acc_copy.wait()
+    shrink = acc[...] + acc_in[...]
+    peers = downs.shape[0]
+    wide = jnp.concatenate([shrink] * (peers * rank // shrink.shape[1]), axis=1)
+    at = lax.broadcasted_iota(jnp.int32, wide.shape, 1)
+    which = (at // rank).astype(jnp.float32)
+    wide = jnp.where(owner == which, wide, 0.0)
+    high = wide.astype(jnp.bfloat16)
+    low = (wide - high.astype(jnp.float32)).astype(jnp.bfloat16)
+    upper = ups[...].reshape(peers * rank, half)
+    delta = jnp.dot(high, upper, preferred_element_type=jnp.float32)
+    delta += jnp.dot(low, upper, preferred_element_type=jnp.float32)
+    out_ref[...] = (mine[...] + delta).astype(out_ref.dtype)
+
+
+def moved_adapters(tokens, value_weight, pool_down, pool_up, block_adapter, pool_slot):
+    peers = lax.axis_size("dp")
+    rows, width = tokens.shape
+    blocks = block_adapter.shape[0]
+    rank = pool_down.shape[2]
+    half = value_weight.shape[1] // lax.axis_size("tensor")
+    down = jnp.swapaxes(pool_down[0], 0, 1)
+    dma = pltpu.SemaphoreType.DMA
+    hbm = pl.BlockSpec(memory_space=pl.ANY)
+    flops = 2 * rows * width * 2 * half * 3
+    return pl.pallas_call(
+        kernel,
+        out_shape=jax.ShapeDtypeStruct((rows, half), jnp.bfloat16),
+        in_specs=[hbm, hbm, hbm, hbm, pl.BlockSpec(memory_space=pltpu.VMEM),
+                  pl.BlockSpec(memory_space=pltpu.SMEM)],
+        out_specs=pl.BlockSpec(memory_space=pltpu.VMEM),
+        scratch_shapes=[
+            pltpu.VMEM((rows, width), jnp.bfloat16),
+            pltpu.VMEM((2, width, half), jnp.bfloat16),
+            pltpu.VMEM((peers, rank, width), jnp.bfloat16),
+            pltpu.VMEM((peers, rank, half), jnp.bfloat16),
+            pltpu.VMEM((rows, half), jnp.float32),
+            pltpu.VMEM((rows, half), jnp.float32),
+            pltpu.VMEM((rows, half), jnp.float32),
+            pltpu.VMEM((rows, 2 * rank), jnp.float32),
+            pltpu.VMEM((rows, 2 * rank), jnp.float32),
+            dma((5,)), dma((peers,)), dma((peers,)), dma((peers,)), dma((peers,)),
+            dma((3, peers)), dma((3, peers)), dma((3, peers)), dma((peers,)),
+            dma((2,)), dma((2,)),
+        ],
+        compiler_params=pltpu.CompilerParams(
+            collective_id=0, has_side_effects=True, vmem_limit_bytes=44 * 2**20),
+        cost_estimate=pl.CostEstimate(flops=flops, bytes_accessed=2 * (rows * width + width * 2 * half), transcendentals=0),
+    )(tokens, value_weight, down, pool_up[0], block_adapter.reshape(1, blocks), pool_slot)
+
+
 def solution(mesh):
     in_specs = (
         P(("rep", "dp"), "tensor"),
@@ -54,4 +331,6 @@
         P(),
     )
     out_specs = P(("rep", "dp"), "tensor")
-    return jax.shard_map(shards, mesh=mesh, in_specs=in_specs, out_specs=out_specs, check_vma=False)
+    fits = mesh.shape["dp"] == 2 * LINE and mesh.shape["rep"] == 2 and mesh.shape["tensor"] == 2
+    body = moved_adapters if fits else moved_tokens
+    return jax.shard_map(body, mesh=mesh, in_specs=in_specs, out_specs=out_specs, check_vma=False)

time: 182 us -> 56 us (0.31)
  blocking collectives: 89.2 us -> 0 us
  Pallas kernels: 0 us -> 49.7 us
  waiting for transfers between devices: 30.6 us -> 0 us
  local copies, waits for them, and re-layouts: 25.4 us -> 6.06 us
  matrix products: 14 us -> 0 us
  between operations: 13.5 us -> 0.01 us
  starting transfers between devices: 6.01 us -> 0 us
  other arithmetic: 3.11 us -> 0 us
    all_to_all x1 -> x0, blocking collectives: 89.2 us -> none  [shards(): lax.all_to_all(outgoing, 'dp', split_axis=0, concat_axis=0, tiled=True)]
    pallas_call x0 -> x1, Pallas kernels: none -> 49.7 us  [moved_adapters(): pl.pallas_call(kernel, out_shape=jax.ShapeDtypeStruct((rows, half), jnp.b...]
    all_to_all x1 -> x0, waiting for transfers between devices: 23.2 us -> none  [shards(): lax.all_to_all(term, 'dp', split_axis=0, concat_axis=0, tiled=True)]
    reshape x3 -> x0, local copies, waits for them, and re-layouts: 15 us -> none  [the longest x1 7.31 us: shards(): flat_blocks = tokens.reshape(blocks, rows_in * width)]
    dot_general x3 -> x0, matrix products: 14 us -> none  [the longest x1 9.7 us: shards(): base = jnp.dot(tokens, value_weight, preferred_element_type=jnp.float32)]
    scatter x1 -> x0, local copies, waits for them, and re-layouts: 8.98 us -> none  [shards(): jnp.zeros((peers * most, rows_in * width), jnp.bfloat16).at[target]]
    psum x1 -> x0, waiting for transfers between devices: 7.33 us -> none  [shards(): shrink_all = lax.psum(shrink_part, 'tensor')]
    unnamed x4 -> x11, local copies, waits for them, and re-layouts: 0.01 us -> 6.06 us
  transfers between devices with their start and end apart: 3 -> 0, of which waited for: 2 -> 0; matrix products, arithmetic and copies ran while one was open for 8% -> 0% of each run, Pallas kernels for 0% -> 0%
where the time goes in v1:
time: 56 us; the launch traced here: 55.8 us
  Pallas kernels  49.7 us (89%)
  local copies, waits for them, and re-layouts  6.06 us (11%)
    pallas_call x1, Pallas kernels, moved_adapters(): pl.pallas_call(kernel, out_shape=jax.ShapeDtypeStruct((rows, half), jnp.b...  49.7 us
    unnamed x11, local copies, waits for them, and re-layouts  6.06 us

profile of v1, /device:TPU:0, one launch (start us, length us, event | category | flops | bytes accessed | tf_op | source)
XLA Modules:
  0.0 55.8 jit_solution(10764531353558950925)
XLA Ops:
  0.0 0.0 copy-start
  0.0 2.0 %copy-done = bf16[448,4096]{1,0:T(8,128)(2,1)S(1)} copy-done((bf16[448,4096]{1,0:T(8,128)(2,1)S(1)}, bf16[448,4096]{1,0:T(8,128)(2,1)}, u32[]{:S(2)}) %copy-start) | copy-done | bytes 3670040
  2.0 0.0 copy-start.1
  2.0 1.0 %copy-done.1 = bf16[1,4096,64]{1,2,0:T(8,128)(2,1)S(1)} copy-done((bf16[1,4096,64]{1,2,0:T(8,128)(2,1)S(1)}, bf16[1,4096,64]{1,2,0:T(8,128)(2,1)}, u32[]{:S(2)}) %copy-start.1) | copy-done | bytes 524312
  3.1 0.0 copy-start.2
  3.1 0.9 %copy-done.2 = bf16[1,64,1024]{2,1,0:T(8,128)(2,1)S(1)} copy-done((bf16[1,64,1024]{2,1,0:T(8,128)(2,1)S(1)}, bf16[1,64,1024]{2,1,0:T(8,128)(2,1)}, u32[]{:S(2)}) %copy-start.2) | copy-done | bytes 131096
  4.0 0.0 copy-start.3
  4.0 0.7 %copy-done.3 = s32[112,1]{0,1:T(1,128)S(1)} copy-done((s32[112,1]{0,1:T(1,128)S(1)}, s32[112,1]{0,1:T(1,128)}, u32[]{:S(2)}) %copy-start.3) | copy-done | bytes 472
  4.6 0.0 copy-start.4
  4.6 0.7 %copy-done.4 = s32[8]{0:T(128)S(1)} copy-done((s32[8]{0:T(128)S(1)}, s32[8]{0:T(128)}, u32[]{:S(2)}) %copy-start.4) | copy-done | bytes 56
  5.3 49.7 %shard_map.64 = bf16[448,512]{1,0:T(8,128)(2,1)S(1)} custom-call(bf16[448,4096]{1,0:T(8,128)(2,1)S(1)} %copy-done, bf16[4096,1024]{1,0:T(8,128)(2,1)} %w_hbm.1, bf16[64,4096]{1,0:T(8,128)(2,1)S(1)} %bitcast.5, bf16[64,1024]{1,0:T(8,128)(2,1)S(1)} %bitcast.6, s32[1,112]{1,0:T(1,128)S(1)} %bitcast.7, s32[8]{0:T(128)S(1)} %copy-done.4), custom_call_target="tpu_custom_call" | custom-call | flops 11274289152 | bytes 12058624 | tf_op jit(solution)/shard_map/pallas_call | solution.py:298
  55.0 0.8 %copy.8 = bf16[448,512]{1,0:T(8,128)(2,1)} copy(bf16[448,512]{1,0:T(8,128)(2,1)S(1)} %shard_map.64) | data formatting | bytes 917504
Async XLA Ops:
  0.0 2.0 %copy-start = (bf16[448,4096]{1,0:T(8,128)(2,1)S(1)}, bf16[448,4096]{1,0:T(8,128)(2,1)}, u32[]{:S(2)}) copy-start(bf16[448,4096]{1,0:T(8,128)(2,1)} %tok_hbm.1) | copy-start | bytes 11010052
  2.0 1.0 %copy-start.1 = (bf16[1,4096,64]{1,2,0:T(8,128)(2,1)S(1)}, bf16[1,4096,64]{1,2,0:T(8,128)(2,1)}, u32[]{:S(2)}) copy-start(bf16[1,4096,64]{1,2,0:T(8,128)(2,1)} %param.8) | copy-start | bytes 1572868
  3.1 0.9 %copy-start.2 = (bf16[1,64,1024]{2,1,0:T(8,128)(2,1)S(1)}, bf16[1,64,1024]{2,1,0:T(8,128)(2,1)}, u32[]{:S(2)}) copy-start(bf16[1,64,1024]{2,1,0:T(8,128)(2,1)} %param.9) | copy-start | bytes 393220
  4.0 0.7 %copy-start.3 = (s32[112,1]{0,1:T(1,128)S(1)}, s32[112,1]{0,1:T(1,128)}, u32[]{:S(2)}) copy-start(s32[112,1]{0,1:T(1,128)} %param.10) | copy-start | bytes 1348
  4.6 0.7 %copy-start.4 = (s32[8]{0:T(128)S(1)}, s32[8]{0:T(128)}, u32[]{:S(2)}) copy-start(s32[8]{0:T(128)} %slot_ref.1) | copy-start | bytes 100

commit v2 on v1

--- a/solution.py
+++ b/solution.py
@@ -51,8 +51,8 @@
     return result.astype(jnp.bfloat16)
 
 
-def kernel(tok_hbm, w_hbm, down_hbm, up_hbm, adapter_ref, slot_ref, out_ref,
-           tok, w, downs, ups, mine, other, base_in, acc, acc_in,
+def kernel(tok_hbm, w_hbm, down_hbm, up_hbm, adapter_hbm, slot_hbm, out_ref,
+           adapter_ref, slot_ref, tok, w, downs, ups, mine, other, base_in, acc, acc_in, last, last_in,
            local_sem, p_recv, c_recv, u_recv, x_recv, p_send, c_send, u_send, x_send,
            core_send, core_recv):
     x, dp, core = lax.axis_index("rep"), lax.axis_index("dp"), lax.axis_index("tensor")
@@ -78,6 +78,8 @@
         pltpu.make_async_copy(w_hbm.at[:, up_cols], w.at[0], local_sem.at[2]),
         pltpu.make_async_copy(down_hbm, downs.at[dp], local_sem.at[3]),
         pltpu.make_async_copy(up_hbm.at[:, up_cols], ups.at[dp], local_sem.at[4]),
+        pltpu.make_async_copy(adapter_hbm, adapter_ref, local_sem.at[5]),
+        pltpu.make_async_copy(slot_hbm, slot_ref, local_sem.at[6]),
     ]
 
     has_up, has_low = z < LINE - 1, z > 0
@@ -85,6 +87,8 @@
     to_up = {"dp": jnp.minimum(dp + 2, 2 * LINE - 1)}
     to_low = {"dp": jnp.maximum(dp - 2, 0)}
 
+    for load in loads:
+        load.start()
     barrier = pltpu.get_barrier_semaphore()
     for near in (to_x, to_y, to_core):
         pl.semaphore_signal(barrier, inc=1, device_id=near, device_id_type=MESH)
@@ -97,8 +101,6 @@
     def _():
         pl.semaphore_signal(barrier, inc=1, device_id=to_low, device_id_type=MESH)
 
-    for load in loads:
-        load.start()
     pl.semaphore_wait(barrier, 3 + jnp.where(has_up, 1, 0) + jnp.where(has_low, 1, 0))
 
     def p_copy(s, way, to, own=False):
@@ -145,8 +147,8 @@
 
     def send_c(s, source_z, own=False):
         def both(way, to):
+            u_copy(s, way, to, own).start()
             c_copy(s, way, to, own).start()
-            u_copy(s, way, to, own).start()
         zs(s, source_z, both)
         both(2, to_y)
 
@@ -154,8 +156,8 @@
         p_copy(s, 2, to_y).wait_recv()
 
     def got_c(s):
+        u_copy(s, 2, to_y).wait_recv()
         c_copy(s, 2, to_y).wait_recv()
-        u_copy(s, 2, to_y).wait_recv()
 
     near = [v * 2 + y for v in line]
     beyond = [v * 2 + 1 - y for v in line]
@@ -163,6 +165,8 @@
 
     send_p(dp, z, True)
     send_c(dp, z, True)
+    for load in loads[5:]:
+        load.wait()
 
     ids = jnp.broadcast_to(adapter_ref[...], (8, blocks))
     own_row = jnp.zeros((8, blocks), jnp.float32)
@@ -180,8 +184,11 @@
         return lax.dot_general(tok[:, cols], both, (((1,), (1,)), ((), ())),
                                preferred_element_type=jnp.float32)
 
-    def add(s, cols):
-        acc[...] += jnp.where(owner == s.astype(jnp.float32), dot_cols(s, cols), 0.0)
+    def add(s, cols, into=acc):
+        into[...] += jnp.where(owner == s.astype(jnp.float32), dot_cols(s, cols), 0.0)
+
+    def exchange(src, dst, at):
+        return pltpu.make_async_remote_copy(src, dst, core_send.at[at], core_recv.at[at], to_core, MESH)
 
     everything = pl.ds(0, width)
     step = width // 8
@@ -196,42 +203,59 @@
         lax.fori_loop(1, 8, body, 0)
 
     acc[...] = jnp.zeros_like(acc)
-    for load in loads:
+    for load in loads[:5]:
         load.wait()
 
-    got_p(near[0])
-    send_p(near[0], line[0])
-    x_copy(near[0]).start()
+    def take_p(i):
+        got_p(near[i])
+        send_p(near[i], line[i])
+        x_copy(near[i]).start()
+
+    def take_c(i):
+        got_c(near[i])
+        send_c(near[i], line[i])
+
+    take_p(0)
     got_p(twin)
     x_copy(twin).start()
+
+    @pl.when(has_up & has_low)
+    def _():
+        take_p(1)
+
     base(other, 1)
-    base_copy = pltpu.make_async_remote_copy(other, base_in, core_send.at[0], core_recv.at[0], to_core, MESH)
+    base_copy = exchange(other, base_in, 0)
     base_copy.start()
-    got_c(near[0])
-    send_c(near[0], line[0])
+    take_c(0)
+
+    @pl.when(has_up & has_low)
+    def _():
+        take_c(1)
+
     base(mine, 0)
 
-    got_p(near[1])
-    send_p(near[1], line[1])
-    x_copy(near[1]).start()
+    @pl.when(jnp.logical_not(has_up & has_low))
+    def _():
+        take_p(1)
+
+    got_p(beyond[0])
+    x_copy(beyond[0]).start()
     add(dp, everything)
     got_c(twin)
-    got_p(beyond[0])
-    x_copy(beyond[0]).start()
-    got_c(near[1])
-    send_c(near[1], line[1])
+
+    @pl.when(jnp.logical_not(has_up & has_low))
+    def _():
+        take_c(1)
+
     x_wait(near[0])
     add(near[0], everything)
 
-    got_p(near[2])
-    send_p(near[2], line[2])
-    x_copy(near[2]).start()
+    take_p(2)
     got_p(beyond[1])
     x_copy(beyond[1]).start()
-    got_c(near[2])
-    send_c(near[2], line[2])
     x_wait(twin)
     add(twin, everything)
+    take_c(2)
     x_wait(near[1])
     add(near[1], everything)
     got_p(beyond[2])
@@ -245,16 +269,34 @@
     got_c(beyond[1])
     x_wait(beyond[1])
     add(beyond[1], everything)
-    add(beyond[2], own_cols)
+    acc_copy = exchange(acc, acc_in, 1)
+    acc_copy.start()
+    last[...] = jnp.zeros_like(last)
+    add(beyond[2], own_cols, last)
     base_copy.wait()
     mine[...] += base_in[...]
-    got_c(beyond[2])
-    add(beyond[2], rest_cols)
+    u_copy(beyond[2], 2, to_y).wait_recv()
+    acc_copy.wait()
+
+    def halves(value):
+        high = value.astype(jnp.bfloat16)
+        return high, (value - high.astype(jnp.float32)).astype(jnp.bfloat16)
+
+    shrink = acc[...] + acc_in[...]
+    peers = downs.shape[0]
+    wide = jnp.concatenate([shrink] * (peers * rank // shrink.shape[1]), axis=1)
+    which = (lax.broadcasted_iota(jnp.int32, wide.shape, 1) // rank).astype(jnp.float32)
+    high, low = halves(jnp.where(owner == which, wide, 0.0))
+    upper = ups[...].reshape(peers * rank, half)
+    mine[...] += jnp.dot(high, upper, preferred_element_type=jnp.float32)
+    mine[...] += jnp.dot(low, upper, preferred_element_type=jnp.float32)
+
+    c_copy(beyond[2], 2, to_y).wait_recv()
+    add(beyond[2], rest_cols, last)
     x_wait(beyond[2])
-    add(beyond[2], far_cols)
-
-    acc_copy = pltpu.make_async_remote_copy(acc, acc_in, core_send.at[1], core_recv.at[1], to_core, MESH)
-    acc_copy.start()
+    add(beyond[2], far_cols, last)
+    last_copy = exchange(last, last_in, 2)
+    last_copy.start()
 
     def sent(s, source_z, own=False):
         def each(way, to):
@@ -270,18 +312,12 @@
     for s in near + beyond + [twin]:
         x_copy(s).wait_send()
 
-    acc_copy.wait()
-    shrink = acc[...] + acc_in[...]
-    peers = downs.shape[0]
-    wide = jnp.concatenate([shrink] * (peers * rank // shrink.shape[1]), axis=1)
-    at = lax.broadcasted_iota(jnp.int32, wide.shape, 1)
-    which = (at // rank).astype(jnp.float32)
-    wide = jnp.where(owner == which, wide, 0.0)
-    high = wide.astype(jnp.bfloat16)
-    low = (wide - high.astype(jnp.float32)).astype(jnp.bfloat16)
-    upper = ups[...].reshape(peers * rank, half)
-    delta = jnp.dot(high, upper, preferred_element_type=jnp.float32)
-    delta += jnp.dot(low, upper, preferred_element_type=jnp.float32)
+    last_copy.wait()
+    high, low = halves(last[...] + last_in[...])
+    row = ups[beyond[2]]
+    left = lax.broadcasted_iota(jnp.int32, high.shape, 1) < rank
+    both = jnp.where(left, high.astype(jnp.float32), low.astype(jnp.float32)).astype(jnp.bfloat16)
+    delta = jnp.dot(both, jnp.concatenate([row, row], axis=0), preferred_element_type=jnp.float32)
     out_ref[...] = (mine[...] + delta).astype(out_ref.dtype)
 
 
@@ -293,15 +329,16 @@
     half = value_weight.shape[1] // lax.axis_size("tensor")
     down = jnp.swapaxes(pool_down[0], 0, 1)
     dma = pltpu.SemaphoreType.DMA
-    hbm = pl.BlockSpec(memory_space=pl.ANY)
+    hbm = pl.BlockSpec(memory_space=pltpu.HBM)
     flops = 2 * rows * width * 2 * half * 3
     return pl.pallas_call(
         kernel,
         out_shape=jax.ShapeDtypeStruct((rows, half), jnp.bfloat16),
-        in_specs=[hbm, hbm, hbm, hbm, pl.BlockSpec(memory_space=pltpu.VMEM),
-                  pl.BlockSpec(memory_space=pltpu.SMEM)],
+        in_specs=[hbm] * 6,
         out_specs=pl.BlockSpec(memory_space=pltpu.VMEM),
         scratch_shapes=[
+            pltpu.VMEM((1, blocks), jnp.int32),
+            pltpu.SMEM(pool_slot.shape, jnp.int32),
             pltpu.VMEM((rows, width), jnp.bfloat16),
             pltpu.VMEM((2, width, half), jnp.bfloat16),
             pltpu.VMEM((peers, rank, width), jnp.bfloat16),
@@ -311,12 +348,14 @@
             pltpu.VMEM((rows, half), jnp.float32),
             pltpu.VMEM((rows, 2 * rank), jnp.float32),
             pltpu.VMEM((rows, 2 * rank), jnp.float32),
-            dma((5,)), dma((peers,)), dma((peers,)), dma((peers,)), dma((peers,)),
+            pltpu.VMEM((rows, 2 * rank), jnp.float32),
+            pltpu.VMEM((rows, 2 * rank), jnp.float32),
+            dma((7,)), dma((peers,)), dma((peers,)), dma((peers,)), dma((peers,)),
             dma((3, peers)), dma((3, peers)), dma((3, peers)), dma((peers,)),
-            dma((2,)), dma((2,)),
+            dma((3,)), dma((3,)),
         ],
         compiler_params=pltpu.CompilerParams(
-            collective_id=0, has_side_effects=True, vmem_limit_bytes=44 * 2**20),
+            collective_id=0, has_side_effects=True, vmem_limit_bytes=64 * 2**20 - 2**16),
         cost_estimate=pl.CostEstimate(flops=flops, bytes_accessed=2 * (rows * width + width * 2 * half), transcendentals=0),
     )(tokens, value_weight, down, pool_up[0], block_adapter.reshape(1, blocks), pool_slot)
 

time: 56 us -> 51.6 us (0.921)
  local copies, waits for them, and re-layouts: 6.06 us -> 1.82 us
    unnamed x11 -> x1, local copies, waits for them, and re-layouts: 6.06 us -> 1.82 us
where the time goes in v2:
time: 51.6 us; the launch traced here: 51.5 us
  Pallas kernels  49.6 us (96%)
  local copies, waits for them, and re-layouts  1.82 us (4%)
    pallas_call x1, Pallas kernels, moved_adapters(): pl.pallas_call(kernel, out_shape=jax.ShapeDtypeStruct((rows, half), jnp.b...  49.6 us
    unnamed x1, local copies, waits for them, and re-layouts  1.82 us

profile of v2, /device:TPU:0, one launch (start us, length us, event | category | flops | bytes accessed | tf_op | source)
XLA Modules:
  0.0 51.5 jit_solution(4490868302167243146)
XLA Ops:
  0.0 49.6 %shard_map.64 = bf16[448,512]{1,0:T(8,128)(2,1)} custom-call(bf16[448,4096]{1,0:T(8,128)(2,1)} %tok_hbm.1, bf16[4096,1024]{1,0:T(8,128)(2,1)} %w_hbm.1, bf16[64,4096]{1,0:T(8,128)(2,1)} %bitcast.5, bf16[64,1024]{1,0:T(8,128)(2,1)} %bitcast.6, s32[1,112]{1,0:T(1,128)} %bitcast.7, s32[8]{0:T(128)} %slot_hbm.1), custom_call_target="tpu_custom_call" | custom-call | flops 11274289152 | bytes 12058624 | tf_op jit(solution)/shard_map/pallas_call | solution.py:334
  49.6 1.8 %copy.8 = bf16[448,512]{1,0:T(8,128)(2,1)} copy(bf16[448,512]{1,0:T(8,128)(2,1)} %shard_map.64) | data formatting | bytes 917504

commit v3 on v2

--- a/solution.py
+++ b/solution.py
@@ -142,15 +142,15 @@
         line.append(jnp.where(z < LINE // 2, rising, falling))
 
     def send_p(s, source_z, own=False):
+        p_copy(s, 2, to_y, own).start()
         zs(s, source_z, lambda way, to: p_copy(s, way, to, own).start())
-        p_copy(s, 2, to_y, own).start()
 
     def send_c(s, source_z, own=False):
         def both(way, to):
             u_copy(s, way, to, own).start()
             c_copy(s, way, to, own).start()
+        both(2, to_y)
         zs(s, source_z, both)
-        both(2, to_y)
 
     def got_p(s):
         p_copy(s, 2, to_y).wait_recv()
@@ -208,8 +208,8 @@
 
     def take_p(i):
         got_p(near[i])
+        x_copy(near[i]).start()
         send_p(near[i], line[i])
-        x_copy(near[i]).start()
 
     def take_c(i):
         got_c(near[i])
@@ -232,8 +232,6 @@
     def _():
         take_c(1)
 
-    base(mine, 0)
-
     @pl.when(jnp.logical_not(has_up & has_low))
     def _():
         take_p(1)
@@ -253,6 +251,7 @@
     take_p(2)
     got_p(beyond[1])
     x_copy(beyond[1]).start()
+    base(mine, 0)
     x_wait(twin)
     add(twin, everything)
     take_c(2)

time: 51.6 us -> 51.3 us (level)
  no operation moved by 1% of the time
where the time goes in v3:
time: 51.3 us; the launch traced here: 51.2 us
  Pallas kernels  49.4 us (96%)
  local copies, waits for them, and re-layouts  1.82 us (4%)
    pallas_call x1, Pallas kernels, moved_adapters(): pl.pallas_call(kernel, out_shape=jax.ShapeDtypeStruct((rows, half), jnp.b...  49.4 us
    unnamed x1, local copies, waits for them, and re-layouts  1.82 us

profile of v3, /device:TPU:0, one launch (start us, length us, event | category | flops | bytes accessed | tf_op | source)
XLA Modules:
  0.0 51.2 jit_solution(1507222836788727030)
XLA Ops:
  0.0 49.4 %shard_map.64 = bf16[448,512]{1,0:T(8,128)(2,1)} custom-call(bf16[448,4096]{1,0:T(8,128)(2,1)} %tok_hbm.1, bf16[4096,1024]{1,0:T(8,128)(2,1)} %w_hbm.1, bf16[64,4096]{1,0:T(8,128)(2,1)} %bitcast.5, bf16[64,1024]{1,0:T(8,128)(2,1)} %bitcast.6, s32[1,112]{1,0:T(1,128)} %bitcast.7, s32[8]{0:T(128)} %slot_hbm.1), custom_call_target="tpu_custom_call" | custom-call | flops 11274289152 | bytes 12058624 | tf_op jit(solution)/shard_map/pallas_call | solution.py:333
  49.4 1.8 %copy.8 = bf16[448,512]{1,0:T(8,128)(2,1)} copy(bf16[448,512]{1,0:T(8,128)(2,1)} %shard_map.64) | data formatting | bytes 917504

commit v4 on v3

--- a/solution.py
+++ b/solution.py
@@ -87,7 +87,7 @@
     to_up = {"dp": jnp.minimum(dp + 2, 2 * LINE - 1)}
     to_low = {"dp": jnp.maximum(dp - 2, 0)}
 
-    for load in loads:
+    for load in loads[3:]:
         load.start()
     barrier = pltpu.get_barrier_semaphore()
     for near in (to_x, to_y, to_core):
@@ -165,6 +165,8 @@
 
     send_p(dp, z, True)
     send_c(dp, z, True)
+    for load in loads[:3]:
+        load.start()
     for load in loads[5:]:
         load.wait()
 

time: 51.3 us -> 51.3 us (level)
  no operation moved by 1% of the time
where the time goes in v4:
time: 51.3 us; the launch traced here: 51.2 us
  Pallas kernels  49.3 us (96%)
  local copies, waits for them, and re-layouts  1.82 us (4%)
    pallas_call x1, Pallas kernels, moved_adapters(): pl.pallas_call(kernel, out_shape=jax.ShapeDtypeStruct((rows, half), jnp.b...  49.3 us
    unnamed x1, local copies, waits for them, and re-layouts  1.82 us

profile of v4, /device:TPU:0, one launch (start us, length us, event | category | flops | bytes accessed | tf_op | source)
XLA Modules:
  0.0 51.2 jit_solution(8099710995578386049)
XLA Ops:
  0.0 49.3 %shard_map.64 = bf16[448,512]{1,0:T(8,128)(2,1)} custom-call(bf16[448,4096]{1,0:T(8,128)(2,1)} %tok_hbm.1, bf16[4096,1024]{1,0:T(8,128)(2,1)} %w_hbm.1, bf16[64,4096]{1,0:T(8,128)(2,1)} %bitcast.5, bf16[64,1024]{1,0:T(8,128)(2,1)} %bitcast.6, s32[1,112]{1,0:T(1,128)} %bitcast.7, s32[8]{0:T(128)} %slot_hbm.1), custom_call_target="tpu_custom_call" | custom-call | flops 11274289152 | bytes 12058624 | tf_op jit(solution)/shard_map/pallas_call | solution.py:335
  49.4 1.8 %copy.8 = bf16[448,512]{1,0:T(8,128)(2,1)} copy(bf16[448,512]{1,0:T(8,128)(2,1)} %shard_map.64) | data formatting | bytes 917504
